TPU v7x, 256 devices: a whole 4x4x8 slice. The times are simulated.
256 devices in a mesh: gy: 8 (over z), gx: 32 (over y, x, core).
Axes of the slice: x: 4, y: 4, z: 8, core: 2. Of those that a mesh axis runs over, the one named last changes fastest.
Arguments:
- increment: float32 [64, 64, 4096], P(None, 'gy', 'gx'), may hold values from -6 to 6
- residual: float32 [64, 64, 4096], P(None, 'gy', 'gx'), as said below
- direction: float32 [64, 64, 4096], P(None, 'gy', 'gx'), as said below
- wind_east: float32 [64, 64, 4096], P(None, 'gy', 'gx'), may hold values from -4 to 4
- wind_north: float32 [64, 64, 4096], P(None, 'gy', 'gx'), may hold values from -4 to 4
- obs_column: int32 [4, 1048576], P(None, ('gy', 'gx')), may hold values from 0 to 1023
- obs_count: int32 [4, 8192], P(None, ('gy', 'gx')), may hold values from 1 to 128, as said below
- obs_weight: float32 [4, 64, 1048576], P(None, None, ('gy', 'gx')), may hold values from 0.25 to 4
Outputs:
- new_increment: float32 [64, 64, 4096], P(None, 'gy', 'gx')
- new_residual: float32 [64, 64, 4096], P(None, 'gy', 'gx')
- new_direction: float32 [64, 64, 4096], P(None, 'gy', 'gx')
Inputs may be any that keep to these rules, and one draw needn't show every extreme that they name: `obs_count`: slots at or past the count are ignored; at every step each owner fills all 128 slots for some grid device. `residual`: a real field. `direction`: a real field.
All inputs are finite; a program needn't handle non-finite values.
Results may differ from a plain program's by a relative error of at most 0.00016.
Values sent between devices are 32-bit elements; how exact they have to be, the bound alone decides.
A program may use at most 128 MiB of HBM per device.

v0:
```python
import functools

import jax
import jax.numpy as jnp
from jax import lax
from jax.experimental import pallas as pl
from jax.experimental.pallas import tpu as pltpu
from jax.sharding import PartitionSpec as P

MESH = pl.DeviceIdType.MESH
F32 = jnp.float32
STEPS = 4
L = 64
ROWS = 8
COLS = 128
CELLS = ROWS * COLS
PLANE = 32
DEPTH = 8
PITCH = 24
LEVELS = L + 2
GROUP = 4
CHUNKS = PLANE // GROUP
OPENING = 10
SENDS = STEPS * (PLANE - 1)

ADVECTION = 0.3
DIFFUSION = 0.1
MIXING = 0.1


def offset_of(slot):
    def far_first(a):
        return 2 - a + (a // 2) * (3 - 2 * (a % 2))

    return far_first(slot // 8), far_first((slot // 2) % 4), 1 - slot % 2


def peer_of(slot):
    me = lax.axis_index("gx")
    dy, dx, dc = offset_of(slot)
    y = (me // 8 + dy) % 4
    x = ((me // 2) % 4 + dx) % 4
    return y * 8 + x * 2 + (me % 2 + dc) % 2


def kernel(
    p_ref, r_ref, we_ref, wn_ref, col_ref, cnt_ref, w_ref,
    h_ref, scal_ref,
    col_send, col_recv, w_recv, w_sum, w_field,
    ext, ext_u, ext_v, abuf,
    row_send, row_recv, edge_send, edge_recv,
    red_send, red_plane, red_mid, red_depth,
    w_ss, w_rs, own_sem, col_ss, col_rs, halo_ss, halo_rs, red_ss, red_rs,
):
    me = lax.axis_index("gx")
    gy = lax.axis_index("gy")
    south, north = (gy + DEPTH - 1) % DEPTH, (gy + 1) % DEPTH
    west, east = (me + PLANE - 1) % PLANE, (me + 1) % PLANE
    lane = lax.broadcasted_iota(jnp.int32, (ROWS, COLS), 1)
    even = lane % 2 == 0
    pair = lane // 2

    barrier = pltpu.get_barrier_semaphore()

    @pl.loop(0, PLANE - 1)
    def _(slot):
        pl.semaphore_signal(barrier, inc=1, device_id={"gx": peer_of(slot)}, device_id_type=MESH)

    @pl.loop(1, DEPTH)
    def _(dz):
        pl.semaphore_signal(barrier, inc=1, device_id={"gy": (gy + dz) % DEPTH}, device_id_type=MESH)

    own = pl.multiple_of(me * COLS, COLS)
    own_copy = pltpu.make_async_copy(w_ref.at[:, :, pl.ds(own, COLS)], w_recv.at[:, PLANE - 1], own_sem)
    own_copy.start()
    slot_id = lax.broadcasted_iota(jnp.int32, (STEPS, COLS), 1)
    counts = cnt_ref[...]
    for g in range(PLANE):
        live = slot_id < counts[:, g : g + 1]
        col_send[g, :STEPS, :] = jnp.where(live, col_ref[:, g * COLS : (g + 1) * COLS], -1)
    col_recv[PLANE - 1] = col_send[me]

    for t in range(STEPS + 1):
        ext[t, 0] = jnp.zeros((PITCH, COLS), F32)
        ext[t, LEVELS - 1] = jnp.zeros((PITCH, COLS), F32)
    for s in range(STEPS):
        abuf[s, 0] = jnp.zeros((ROWS, COLS), F32)
        abuf[s, LEVELS - 1] = jnp.zeros((ROWS, COLS), F32)

    def rolled_edges(field, l, acc):
        return jnp.where(pair == l, pltpu.roll(field, 2 * l + 1, 1), acc)

    def load_level(l, carry):
        edges, rr, pp = carry
        f = p_ref[l]
        r = r_ref[l]
        ext[0, l + 1, 8:16, :] = f
        return rolled_edges(f, l, edges), rr + r * r, pp + f * f

    zero = jnp.zeros((ROWS, COLS), F32)
    edges, rr_part, pp_part = lax.fori_loop(0, L, load_level, (zero, zero, zero), unroll=8)

    pl.semaphore_wait(barrier, PLANE - 1 + DEPTH - 1)

    def col_copy(slot):
        return pltpu.make_async_remote_copy(
            src_ref=col_send.at[peer_of(slot)], dst_ref=col_recv.at[slot],
            send_sem=col_ss.at[slot], recv_sem=col_rs.at[slot],
            device_id={"gx": peer_of(slot)}, device_id_type=MESH,
        )

    def weight_copy(order, slot):
        p = peer_of(slot)
        return pltpu.make_async_remote_copy(
            src_ref=w_ref.at[STEPS - 1 - order, :, pl.ds(pl.multiple_of(p * COLS, COLS), COLS)],
            dst_ref=w_recv.at[STEPS - 1 - order, slot],
            send_sem=w_ss.at[order, slot], recv_sem=w_rs.at[order, slot],
            device_id={"gx": p}, device_id_type=MESH,
        )

    def send_weights(first, count):
        @pl.loop(first, first + count)
        def _(i):
            weight_copy(i // (PLANE - 1), i % (PLANE - 1)).start()

    def halo_copies(k):
        to = ({"gy": south}, {"gy": north}, {"gx": west}, {"gx": east})
        src = (row_send.at[k, 0], row_send.at[k, 1], edge_send.at[k], edge_send.at[k])
        dst = (row_recv.at[k, 1], row_recv.at[k, 0], edge_recv.at[k, 1], edge_recv.at[k, 0])
        return [
            pltpu.make_async_remote_copy(
                src_ref=src[i], dst_ref=dst[i], send_sem=halo_ss.at[k, i], recv_sem=halo_rs.at[k, i],
                device_id=to[i], device_id_type=MESH,
            )
            for i in range(4)
        ]

    def flat(ref, index):
        return ref.at[index].reshape(LEVELS * PITCH, COLS)

    def send_halo(k, low, high, edges):
        row_send[k, 0] = low[pl.ds(PITCH + 8, L, stride=PITCH), :]
        row_send[k, 1] = high[pl.ds(PITCH + 15, L, stride=PITCH), :]
        edge_send[k] = edges
        for copy in halo_copies(k):
            copy.start()

    def take_halo(k, low, high):
        for copy in halo_copies(k):
            copy.wait_recv()
        low[pl.ds(PITCH + 7, L, stride=PITCH), :] = jnp.where(gy > 0, row_recv[k, 0], 0.0)
        high[pl.ds(PITCH + 16, L, stride=PITCH), :] = jnp.where(gy < DEPTH - 1, row_recv[k, 1], 0.0)
        from_west = jnp.where(me > 0, edge_recv[k, 0], 0.0)
        from_east = jnp.where(me < PLANE - 1, edge_recv[k, 1], 0.0)
        return jnp.where(even, pltpu.roll(from_east, COLS - 1, 1), pltpu.roll(from_west, 1, 1))

    for t in range(1, STEPS + 1):
        state = flat(ext, t - 1)
        send_halo(t - 1, state, state, edges)
        if t == 1:
            @pl.loop(0, PLANE - 1)
            def _(slot):
                col_copy(slot).start()
        send_weights((t - 1) * OPENING, OPENING)
        beside = take_halo(t - 1, state, state)

        def tangent_level(l, edges, t=t, beside=beside):
            f = ext[t - 1, l + 1, 8:16, :]
            up = ext[t - 1, l + 1, 9:17, :]
            down = ext[t - 1, l + 1, 7:15, :]
            border = pltpu.roll(beside, COLS - 1 - 2 * l, 1)
            right = jnp.where(lane == COLS - 1, border, pltpu.roll(f, COLS - 1, 1))
            left = jnp.where(lane == 0, border, pltpu.roll(f, 1, 1))
            levels = ext[t - 1, l + 2, 8:16, :] + ext[t - 1, l, 8:16, :]
            out = (
                f
                - ADVECTION * (we_ref[l] * (right - left) + wn_ref[l] * (up - down))
                + DIFFUSION * (up + down + right + left - 4.0 * f)
                + MIXING * (levels - 2.0 * f)
            )
            ext[t, l + 1, 8:16, :] = out
            return rolled_edges(out, l, edges)

        edges = lax.fori_loop(0, L, tangent_level, zero, unroll=8)

    own_copy.wait()

    @pl.loop(0, PLANE - 1)
    def _(slot):
        col_copy(slot).wait_recv()

    cell = lax.broadcasted_iota(jnp.int32, (2 * COLS, GROUP * COLS), 0)

    def add_group(t, group, first):
        weights = jnp.concatenate([w_recv[t, group * GROUP + j] for j in range(GROUP)], axis=1)
        ids = jnp.concatenate([col_recv[group * GROUP + j, t : t + 1, :] for j in range(GROUP)], axis=1)
        high = weights.astype(jnp.bfloat16)
        low = (weights - high.astype(F32)).astype(jnp.bfloat16)
        both = jnp.concatenate([high, low], axis=0)
        for q in range(CELLS // (2 * COLS)):
            chosen = jnp.where(cell == ids - q * 2 * COLS, 1.0, 0.0).astype(jnp.bfloat16)
            part = lax.dot_general(both, chosen, (((1,), (1,)), ((), ())), preferred_element_type=F32)
            here = pl.ds(q * 2 * COLS, 2 * COLS)
            w_sum[:, here] = part if first else w_sum[:, here] + part

    def sum_weights(order):
        t = STEPS - 1 - order

        def one(group, first):
            for j in range(GROUP):
                weight_copy(order, group * GROUP + j).wait_recv()
            number = order * (CHUNKS - 1) + group
            start = STEPS * OPENING + number * GROUP

            @pl.when(start < SENDS)
            def _():
                send_weights(start, GROUP)

            add_group(t, group, first)

        one(0, True)

        @pl.loop(1, CHUNKS - 1)
        def _(group):
            one(group, False)

        for j in range(GROUP - 1):
            weight_copy(order, (CHUNKS - 1) * GROUP + j).wait_recv()
        add_group(t, CHUNKS - 1, False)
        field = w_field.reshape(L * ROWS, COLS)
        for r in range(ROWS):
            here = pl.ds(r * COLS, COLS)
            field[pl.ds(r, L, stride=ROWS), :] = w_sum[:L, here] + w_sum[L:, here]

    def adjoint_of(s, l, beside):
        a = abuf[s, l + 1]
        border = pltpu.roll(beside, COLS - 1 - 2 * l, 1)
        we = ADVECTION * we_ref[l]
        right = jnp.where(lane == COLS - 1, border, pltpu.roll((DIFFUSION + we) * a, COLS - 1, 1))
        left = jnp.where(lane == 0, border, pltpu.roll((DIFFUSION - we) * a, 1, 1))
        up = ext_u[s, l + 1, 9:17, :]
        down = ext_v[s, l + 1, 7:15, :]
        centre = 1.0 - 4.0 * DIFFUSION - 2.0 * MIXING
        return centre * a + (right + left) + (up + down) + MIXING * (abuf[s, l + 2] + abuf[s, l])

    pq_part = pp_part
    beside = None
    for order in range(STEPS):
        sum_weights(order)
        if order:
            beside = take_halo(STEPS + order - 1, flat(ext_v, order - 1), flat(ext_u, order - 1))

        def adjoint_level(l, carry, order=order, beside=beside):
            edges, pq = carry
            state = ext[STEPS - order, l + 1, 8:16, :]
            forcing = w_field[l] * state
            a = forcing + adjoint_of(order - 1, l, beside) if order else forcing
            we = ADVECTION * we_ref[l]
            wn = ADVECTION * wn_ref[l]
            abuf[order, l + 1] = a
            ext_u[order, l + 1, 8:16, :] = (DIFFUSION + wn) * a
            ext_v[order, l + 1, 8:16, :] = (DIFFUSION - wn) * a
            sent = jnp.where(lane == COLS - 1, DIFFUSION - we, DIFFUSION + we) * a
            return rolled_edges(sent, l, edges), pq + forcing * state

        edges, pq_part = lax.fori_loop(0, L, adjoint_level, (zero, pq_part), unroll=8)
        send_halo(STEPS + order, flat(ext_u, order), flat(ext_v, order), edges)

    def plane_copy(k, slot):
        return pltpu.make_async_remote_copy(
            src_ref=red_send.at[k], dst_ref=red_plane.at[k, slot],
            send_sem=red_ss.at[k, slot], recv_sem=red_rs.at[k, slot],
            device_id={"gx": peer_of(slot)}, device_id_type=MESH,
        )

    def depth_copy(k, dz):
        return pltpu.make_async_remote_copy(
            src_ref=red_mid.at[k], dst_ref=red_depth.at[k, dz - 1],
            send_sem=red_ss.at[k, PLANE - 1 + dz], recv_sem=red_rs.at[k, PLANE - 1 + dz],
            device_id={"gy": (gy + dz) % DEPTH}, device_id_type=MESH,
        )

    def reduce_start(k, value):
        red_send[k] = value

        @pl.loop(0, PLANE - 1)
        def _(slot):
            plane_copy(k, slot).start()

    def reduce_finish(k):
        @pl.loop(0, PLANE - 1)
        def _(slot):
            plane_copy(k, slot).wait_recv()

        total = red_send[k]
        for slot in range(PLANE - 1):
            total = total + red_plane[k, slot]
        red_mid[k] = total
        for dz in range(1, DEPTH):
            depth_copy(k, dz).start()
        for dz in range(1, DEPTH):
            depth_copy(k, dz).wait_recv()
        for dz in range(1, DEPTH):
            total = total + red_depth[k, dz - 1]
        return total

    row = lax.broadcasted_iota(jnp.int32, (ROWS, COLS), 0)
    upper = row < ROWS // 2
    rr_half = rr_part + pltpu.roll(rr_part, ROWS // 2, 0)
    pq_half = pq_part + pltpu.roll(pq_part, ROWS // 2, 0)
    reduce_start(0, jnp.where(upper, rr_half, pq_half))
    beside = take_halo(2 * STEPS - 1, flat(ext_v, STEPS - 1), flat(ext_u, STEPS - 1))

    def hessian_level(l, carry):
        h_ref[l] = p_ref[l] + adjoint_of(STEPS - 1, l, beside)
        return carry

    lax.fori_loop(0, L, hessian_level, 0, unroll=8)
    both = reduce_finish(0)
    rr = jnp.sum(jnp.where(upper, both, 0.0), axis=(0, 1), keepdims=True)
    pq = jnp.sum(jnp.where(upper, 0.0, both), axis=(0, 1), keepdims=True)
    alpha = jnp.broadcast_to(rr / pq, (ROWS, COLS))

    def residual_level(l, total):
        new = r_ref[l] - alpha * h_ref[l]
        return total + new * new

    reduce_start(1, lax.fori_loop(0, L, residual_level, zero, unroll=8))
    rr_next = jnp.sum(reduce_finish(1), axis=(0, 1), keepdims=True)
    scal_ref[0] = alpha
    scal_ref[1] = jnp.broadcast_to(rr_next / rr, (ROWS, COLS))

    for k in range(2 * STEPS):
        for copy in halo_copies(k):
            copy.wait_send()

    @pl.loop(0, PLANE - 1)
    def _(slot):
        col_copy(slot).wait_send()
        for order in range(STEPS):
            weight_copy(order, slot).wait_send()
        for k in range(2):
            plane_copy(k, slot).wait_send()

    for k in range(2):
        for dz in range(1, DEPTH):
            depth_copy(k, dz).wait_send()


def shards(increment, residual, direction, wind_east, wind_north, obs_column, obs_count, obs_weight):
    vmem = pl.BlockSpec(memory_space=pltpu.VMEM)
    dma = pltpu.SemaphoreType.DMA
    hessian, scalars = pl.pallas_call(
        kernel,
        out_shape=(
            jax.ShapeDtypeStruct((L, ROWS, COLS), F32),
            jax.ShapeDtypeStruct((2, ROWS, COLS), F32),
        ),
        in_specs=[vmem] * 6 + [pl.BlockSpec(memory_space=pl.ANY)],
        out_specs=(vmem, vmem),
        scratch_shapes=[
            pltpu.VMEM((PLANE, 8, COLS), jnp.int32),
            pltpu.VMEM((PLANE, 8, COLS), jnp.int32),
            pltpu.VMEM((STEPS, PLANE, L, COLS), F32),
            pltpu.VMEM((2 * L, CELLS), F32),
            pltpu.VMEM((L, ROWS, COLS), F32),
            pltpu.VMEM((STEPS + 1, LEVELS, PITCH, COLS), F32),
            pltpu.VMEM((STEPS, LEVELS, PITCH, COLS), F32),
            pltpu.VMEM((STEPS, LEVELS, PITCH, COLS), F32),
            pltpu.VMEM((STEPS, LEVELS, ROWS, COLS), F32),
            pltpu.VMEM((2 * STEPS, 2, L, COLS), F32),
            pltpu.VMEM((2 * STEPS, 2, L, COLS), F32),
            pltpu.VMEM((2 * STEPS, ROWS, COLS), F32),
            pltpu.VMEM((2 * STEPS, 2, ROWS, COLS), F32),
            pltpu.VMEM((2, ROWS, COLS), F32),
            pltpu.VMEM((2, PLANE - 1, ROWS, COLS), F32),
            pltpu.VMEM((2, ROWS, COLS), F32),
            pltpu.VMEM((2, DEPTH - 1, ROWS, COLS), F32),
            dma((STEPS, PLANE)), dma((STEPS, PLANE)), dma, dma((PLANE,)), dma((PLANE,)),
            dma((2 * STEPS, 4)), dma((2 * STEPS, 4)),
            dma((2, PLANE + DEPTH)), dma((2, PLANE + DEPTH)),
        ],
        compiler_params=pltpu.CompilerParams(
            collective_id=0, has_side_effects=True, vmem_limit_bytes=40 * 2**20
        ),
    )(direction, residual, wind_east, wind_north, obs_column, obs_count, obs_weight)
    alpha = scalars[0, 0, 0]
    beta = scalars[1, 0, 0]
    new_increment = increment + alpha * direction
    new_residual = residual - alpha * hessian
    new_direction = new_residual + beta * direction
    return new_increment, new_residual, new_direction


def solution(mesh):
    field = P(None, "gy", "gx")
    slots = P(None, ("gy", "gx"))
    return jax.shard_map(
        shards,
        mesh=mesh,
        in_specs=(field, field, field, field, field, slots, slots, P(None, None, ("gy", "gx"))),
        out_specs=(field, field, field),
        check_vma=False,
    )
```

profile of v0, /device:TPU:1, one launch (start us, length us, event | category | flops | bytes accessed | tf_op | source)
XLA Modules:
  0.0 105.7 jit_solution(8245275584413507177)
XLA Ops:
  0.6 0.0 copy-start
  0.6 2.2 %copy-done = f32[4,64,4096]{2,1,0:T(8,128)S(1)} copy-done((f32[4,64,4096]{2,1,0:T(8,128)S(1)}, f32[4,64,4096]{2,1,0:T(8,128)}, u32[]{:S(2)}) %copy-start) | copy-done | bytes 4194328
  2.8 0.0 copy-start.1
  2.8 0.9 copy-done.1
  3.8 0.0 copy-start.2
  3.8 0.9 copy-done.2
  4.7 0.0 copy-start.3
  4.7 0.9 copy-done.3
  5.7 0.0 copy-start.4
  5.7 0.9 copy-done.4
  6.6 0.0 copy-start.5
  6.6 0.8 copy-done.5
  7.5 0.0 copy-start.6
  7.5 0.7 copy-done.6
  8.1 0.0 copy-start.7
  8.1 94.8 %shard_map.103 = (f32[64,8,128]{2,1,0:T(8,128)S(1)}, f32[2,8,128]{2,1,0:T(8,128)S(1)}) custom-call(f32[64,8,128]{2,1,0:T(8,128)S(1)} %copy-done.1, f32[64,8,128]{2,1,0:T(8,128)S(1)} %copy-done.2, f32[64,8,128]{2,1,0:T(8,128)S(1)} %copy-done.3, f32[64,8,128]{2,1,0:T(8,128)S(1)} %copy-done.4, s32[4,4096]{1,0:T(4,128)S(1)} %copy-done.5, s32[4,32]{1,0:T(4,128)S(1)} %copy-done.6, ...), custom_call_target="tpu_custom_call" | custom-call | tf_op jit(solution)/shard_map/pallas_call | solution.py:353
  102.9 0.6 fusion
  103.5 0.0 copy-done.7
  103.5 2.2 %multiply_add_fusion = (f32[64,8,128]{2,1,0:T(8,128)}, f32[64,8,128]{2,1,0:T(8,128)}, f32[64,8,128]{2,1,0:T(8,128)}) fusion(f32[64,8,128]{2,1,0:T(8,128)S(1)} %copy-done.1, f32[]{:T(128)} %bitcast.1, f32[64,8,128]{2,1,0:T(8,128)S(1)} %copy-done.2, f32[64,8,128]{2,1,0:T(8,128)S(1)} %get-tuple-element.6, f32[]{:T(128)} %bitcast, f32[64,8,128]{2,1,0:T(8,128)S(1)} %copy-done.7), kind=kLoop, calls=%fused_computation | loop fusion | flops 393216 | bytes 1835016 | tf_op jit(solution)/shard_map/add | solution.py:391
Async XLA Ops:
  0.6 2.2 %copy-start = (f32[4,64,4096]{2,1,0:T(8,128)S(1)}, f32[4,64,4096]{2,1,0:T(8,128)}, u32[]{:S(2)}) copy-start(f32[4,64,4096]{2,1,0:T(8,128)} %w_ref.1) | copy-start | bytes 12582916
  2.8 0.9 copy-start.1
  3.8 0.9 copy-start.2
  4.7 0.9 copy-start.3
  5.7 0.9 copy-start.4
  6.6 0.8 copy-start.5
  7.5 0.7 copy-start.6
  8.1 95.4 %copy-start.7 = (f32[64,8,128]{2,1,0:T(8,128)S(1)}, f32[64,8,128]{2,1,0:T(8,128)}, u32[]{:S(2)}) copy-start(f32[64,8,128]{2,1,0:T(8,128)} %param.8) | copy-start | bytes 786436
where the time goes:
time: 106 us
  Pallas kernels  94.8 us (89%)
  local copies, waits for them, and re-layouts  8.08 us (8%)
  other arithmetic  2.18 us (2%)
    pallas_call x1, Pallas kernels, shards(): pl.pallas_call(kernel, out_shape=(jax.ShapeDtypeStruct((L, ROWS, COLS), F...  94.8 us
    unnamed x16, local copies, waits for them, and re-layouts  7.5 us
    add x1, other arithmetic, shards(): new_direction = new_residual + beta * direction  2.18 us

commit v1 on v0

v1 whole, which is shorter than its diff:
```python
import functools

import jax
import jax.numpy as jnp
from jax import lax
from jax.experimental import pallas as pl
from jax.experimental.pallas import tpu as pltpu
from jax.sharding import PartitionSpec as P

MESH = pl.DeviceIdType.MESH
F32 = jnp.float32
STEPS = 4
L = 64
ROWS = 8
COLS = 128
CELLS = ROWS * COLS
PLANE = 32
DEPTH = 8
PITCH = 24
LEVELS = L + 2
GROUP = 4
CHUNKS = PLANE // GROUP
OPENING = 10
SENDS = STEPS * (PLANE - 1)

ADVECTION = 0.3
DIFFUSION = 0.1
MIXING = 0.1
SMALL = 2.0**-32


def offset_of(slot):
    def far_first(a):
        return 2 - a + (a // 2) * (3 - 2 * (a % 2))

    return far_first(slot // 8), far_first((slot // 2) % 4), 1 - slot % 2


def peer_of(slot):
    me = lax.axis_index("gx")
    dy, dx, dc = offset_of(slot)
    y = (me // 8 + dy) % 4
    x = ((me // 2) % 4 + dx) % 4
    return y * 8 + x * 2 + (me % 2 + dc) % 2


def two_sum(a, b):
    s = a + b
    t = s - a
    return s, (a - (s - t)) + (b - t)


def halves(a):
    c = 4097.0 * a
    high = c - (c - a)
    return high, a - high


def two_product(a, b):
    p = a * b
    ah, al = halves(a)
    bh, bl = halves(b)
    return p, ((ah * bh - p) + ah * bl + al * bh) + al * bl


def add_product(total, a, b):
    high, low = total
    p, rest = two_product(a, b)
    high, lost = two_sum(high, p)
    return high, low + (lost + rest)


def fold_rows(total):
    high, low = total
    for shift in (4, 2, 1):
        high, lost = two_sum(high, pltpu.roll(high, shift, 0))
        low = low + pltpu.roll(low, shift, 0) + lost
    return high, low


def kernel(
    p_hbm, r_hbm, we_hbm, wn_hbm, col_hbm, cnt_hbm, w_hbm,
    h_ref, alpha_ref, beta_ref,
    p_ref, r_ref, we_ref, wn_ref, col_ref, cnt_ref,
    w_send, w_recv, w_sum, w_field,
    ext, ext_u, ext_v, abuf,
    row_send, row_recv, edge_send, edge_recv,
    red_send, red_plane, red_mid, red_depth,
    in_sem, block_sem, w_ss, w_rs, halo_ss, halo_rs, red_ss, red_rs,
):
    me = lax.axis_index("gx")
    gy = lax.axis_index("gy")
    south, north = (gy + DEPTH - 1) % DEPTH, (gy + 1) % DEPTH
    west, east = (me + PLANE - 1) % PLANE, (me + 1) % PLANE
    lane = lax.broadcasted_iota(jnp.int32, (ROWS, COLS), 1)
    even = lane % 2 == 0
    pair = lane // 2

    loads = [
        pltpu.make_async_copy(src, dst, in_sem.at[i])
        for i, (src, dst) in enumerate((
            (cnt_hbm, cnt_ref), (col_hbm, col_ref), (p_hbm, p_ref),
            (r_hbm, r_ref), (we_hbm, we_ref), (wn_hbm, wn_ref),
        ))
    ]
    for load in loads:
        load.start()

    def block_load(g):
        here = pl.ds(pl.multiple_of(g * COLS, COLS), COLS)
        return pltpu.make_async_copy(w_hbm.at[:, :, here], w_send.at[:, g, pl.ds(0, L)], block_sem.at[g])

    @pl.loop(0, PLANE)
    def _(g):
        block_load(g).start()

    barrier = pltpu.get_barrier_semaphore()

    @pl.loop(0, PLANE - 1)
    def _(slot):
        pl.semaphore_signal(barrier, inc=1, device_id={"gx": peer_of(slot)}, device_id_type=MESH)

    @pl.loop(1, DEPTH)
    def _(dz):
        pl.semaphore_signal(barrier, inc=1, device_id={"gy": (gy + dz) % DEPTH}, device_id_type=MESH)

    loads[0].wait()
    loads[1].wait()
    slot_id = lax.broadcasted_iota(jnp.int32, (STEPS, COLS), 1)
    counts = cnt_ref[...]
    for g in range(PLANE):
        live = slot_id < counts[:, g : g + 1]
        columns = jnp.where(live, col_ref[:, g * COLS : (g + 1) * COLS], -1).astype(F32)
        w_send[STEPS - 1, g, L : L + STEPS, :] = columns
        w_send[STEPS - 1, g, L + STEPS :, :] = columns

    for t in range(STEPS + 1):
        ext[t, 0] = jnp.zeros((PITCH, COLS), F32)
        ext[t, LEVELS - 1] = jnp.zeros((PITCH, COLS), F32)
    for s in range(STEPS):
        abuf[s, 0] = jnp.zeros((ROWS, COLS), F32)
        abuf[s, LEVELS - 1] = jnp.zeros((ROWS, COLS), F32)

    for load in loads[2:]:
        load.wait()

    def rolled_edges(field, l, acc):
        return jnp.where(pair == l, pltpu.roll(field, 2 * l + 1, 1), acc)

    def load_level(l, carry):
        edges, rr, pp = carry
        f = p_ref[l]
        r = r_ref[l]
        ext[0, l + 1, 8:16, :] = f
        return rolled_edges(f, l, edges), add_product(rr, r, r), pp + f * f

    zero = jnp.zeros((ROWS, COLS), F32)
    edges, rr_part, pp_part = lax.fori_loop(0, L, load_level, (zero, (zero, zero), zero), unroll=8)

    @pl.loop(0, PLANE)
    def _(g):
        block_load(g).wait()

    pl.semaphore_wait(barrier, PLANE - 1 + DEPTH - 1)

    def weight_copy(order, slot, height):
        p = peer_of(slot)
        t = STEPS - 1 - order
        return pltpu.make_async_remote_copy(
            src_ref=w_send.at[t, p, pl.ds(0, height)],
            dst_ref=w_recv.at[t, slot, pl.ds(0, height)],
            send_sem=w_ss.at[order, slot], recv_sem=w_rs.at[order, slot],
            device_id={"gx": p}, device_id_type=MESH,
        )

    def height_of(order):
        return L if order else L + ROWS

    def send_weights(first, count):
        @pl.loop(first, first + count)
        def _(i):
            order, slot = i // (PLANE - 1), i % (PLANE - 1)

            @pl.when(order == 0)
            def _():
                weight_copy(0, slot, L + ROWS).start()

            @pl.when(order > 0)
            def _():
                weight_copy(order, slot, L).start()

    def halo_copies(k):
        to = ({"gy": south}, {"gy": north}, {"gx": west}, {"gx": east})
        src = (row_send.at[k, 0], row_send.at[k, 1], edge_send.at[k], edge_send.at[k])
        dst = (row_recv.at[k, 1], row_recv.at[k, 0], edge_recv.at[k, 1], edge_recv.at[k, 0])
        return [
            pltpu.make_async_remote_copy(
                src_ref=src[i], dst_ref=dst[i], send_sem=halo_ss.at[k, i], recv_sem=halo_rs.at[k, i],
                device_id=to[i], device_id_type=MESH,
            )
            for i in range(4)
        ]

    def flat(ref, index):
        return ref.at[index].reshape(LEVELS * PITCH, COLS)

    def send_halo(k, low, high, edges):
        row_send[k, 0] = low[pl.ds(PITCH + 8, L, stride=PITCH), :]
        row_send[k, 1] = high[pl.ds(PITCH + 15, L, stride=PITCH), :]
        edge_send[k] = edges
        for copy in halo_copies(k):
            copy.start()

    def take_halo(k, low, high):
        for copy in halo_copies(k):
            copy.wait_recv()
        low[pl.ds(PITCH + 7, L, stride=PITCH), :] = jnp.where(gy > 0, row_recv[k, 0], 0.0)
        high[pl.ds(PITCH + 16, L, stride=PITCH), :] = jnp.where(gy < DEPTH - 1, row_recv[k, 1], 0.0)
        from_west = jnp.where(me > 0, edge_recv[k, 0], 0.0)
        from_east = jnp.where(me < PLANE - 1, edge_recv[k, 1], 0.0)
        return jnp.where(even, pltpu.roll(from_east, COLS - 1, 1), pltpu.roll(from_west, 1, 1))

    for t in range(1, STEPS + 1):
        state = flat(ext, t - 1)
        send_halo(t - 1, state, state, edges)
        send_weights((t - 1) * OPENING, OPENING)
        beside = take_halo(t - 1, state, state)

        def tangent_level(l, edges, t=t, beside=beside):
            f = ext[t - 1, l + 1, 8:16, :]
            up = ext[t - 1, l + 1, 9:17, :]
            down = ext[t - 1, l + 1, 7:15, :]
            border = pltpu.roll(beside, COLS - 1 - 2 * l, 1)
            right = jnp.where(lane == COLS - 1, border, pltpu.roll(f, COLS - 1, 1))
            left = jnp.where(lane == 0, border, pltpu.roll(f, 1, 1))
            levels = ext[t - 1, l + 2, 8:16, :] + ext[t - 1, l, 8:16, :]
            out = (
                f
                - ADVECTION * (we_ref[l] * (right - left) + wn_ref[l] * (up - down))
                + DIFFUSION * (up + down + right + left - 4.0 * f)
                + MIXING * (levels - 2.0 * f)
            )
            ext[t, l + 1, 8:16, :] = out
            return rolled_edges(out, l, edges)

        edges = lax.fori_loop(0, L, tangent_level, zero, unroll=8)

    cell = lax.broadcasted_iota(jnp.int32, (2 * COLS, GROUP * COLS), 0).astype(F32)

    def add_group(t, group, own, first):
        slots = [group * GROUP + j for j in range(GROUP)]
        blocks = [w_recv.at[t, slot] for slot in slots]
        columns = [w_recv.at[STEPS - 1, slot] for slot in slots]
        if own:
            blocks[-1], columns[-1] = w_send.at[t, me], w_send.at[STEPS - 1, me]
        weights = jnp.concatenate([block[:L, :] for block in blocks], axis=1)
        ids = jnp.concatenate([column[L + t : L + t + 1, :] for column in columns], axis=1)
        high = weights.astype(jnp.bfloat16)
        low = (weights - high.astype(F32)).astype(jnp.bfloat16)
        both = jnp.concatenate([high, low], axis=0)
        for q in range(CELLS // (2 * COLS)):
            chosen = jnp.where(cell == ids - float(q * 2 * COLS), 1.0, 0.0).astype(jnp.bfloat16)
            part = lax.dot_general(both, chosen, (((1,), (1,)), ((), ())), preferred_element_type=F32)
            here = pl.ds(q * 2 * COLS, 2 * COLS)
            w_sum[:, here] = part if first else w_sum[:, here] + part

    def sum_weights(order):
        t = STEPS - 1 - order

        def one(group, first):
            for j in range(GROUP):
                weight_copy(order, group * GROUP + j, height_of(order)).wait_recv()
            number = order * (CHUNKS - 1) + group
            start = STEPS * OPENING + number * GROUP

            @pl.when(start < SENDS)
            def _():
                send_weights(start, GROUP)

            add_group(t, group, False, first)

        one(0, True)

        @pl.loop(1, CHUNKS - 1)
        def _(group):
            one(group, False)

        for j in range(GROUP - 1):
            weight_copy(order, (CHUNKS - 1) * GROUP + j, height_of(order)).wait_recv()
        add_group(t, CHUNKS - 1, True, False)
        field = w_field.reshape(L * ROWS, COLS)
        for r in range(ROWS):
            here = pl.ds(r * COLS, COLS)
            field[pl.ds(r, L, stride=ROWS), :] = w_sum[:L, here] + w_sum[L:, here]

    def adjoint_of(s, l, beside):
        a = abuf[s, l + 1]
        border = pltpu.roll(beside, COLS - 1 - 2 * l, 1)
        we = ADVECTION * we_ref[l]
        right = jnp.where(lane == COLS - 1, border, pltpu.roll((DIFFUSION + we) * a, COLS - 1, 1))
        left = jnp.where(lane == 0, border, pltpu.roll((DIFFUSION - we) * a, 1, 1))
        up = ext_u[s, l + 1, 9:17, :]
        down = ext_v[s, l + 1, 7:15, :]
        centre = 1.0 - 4.0 * DIFFUSION - 2.0 * MIXING
        return centre * a + (right + left) + (up + down) + MIXING * (abuf[s, l + 2] + abuf[s, l])

    pq_part = pp_part
    beside = None
    for order in range(STEPS):
        sum_weights(order)
        if order:
            beside = take_halo(STEPS + order - 1, flat(ext_v, order - 1), flat(ext_u, order - 1))

        def adjoint_level(l, carry, order=order, beside=beside):
            edges, pq = carry
            state = ext[STEPS - order, l + 1, 8:16, :]
            forcing = w_field[l] * state
            a = forcing + adjoint_of(order - 1, l, beside) if order else forcing
            we = ADVECTION * we_ref[l]
            wn = ADVECTION * wn_ref[l]
            abuf[order, l + 1] = a
            ext_u[order, l + 1, 8:16, :] = (DIFFUSION + wn) * a
            ext_v[order, l + 1, 8:16, :] = (DIFFUSION - wn) * a
            sent = jnp.where(lane == COLS - 1, DIFFUSION - we, DIFFUSION + we) * a
            return rolled_edges(sent, l, edges), pq + forcing * state

        edges, pq_part = lax.fori_loop(0, L, adjoint_level, (zero, pq_part), unroll=8)
        send_halo(STEPS + order, flat(ext_u, order), flat(ext_v, order), edges)

    def plane_copy(slot):
        return pltpu.make_async_remote_copy(
            src_ref=red_send, dst_ref=red_plane.at[slot],
            send_sem=red_ss.at[slot], recv_sem=red_rs.at[slot],
            device_id={"gx": peer_of(slot)}, device_id_type=MESH,
        )

    def depth_copy(dz):
        return pltpu.make_async_remote_copy(
            src_ref=red_mid, dst_ref=red_depth.at[dz - 1],
            send_sem=red_ss.at[PLANE - 1 + dz], recv_sem=red_rs.at[PLANE - 1 + dz],
            device_id={"gy": (gy + dz) % DEPTH}, device_id_type=MESH,
        )

    row = lax.broadcasted_iota(jnp.int32, (ROWS, COLS), 0)
    upper = row < ROWS // 2

    def add(a, b):
        total, lost = two_sum(a[0], b[0])
        return jnp.where(upper, total, total + pltpu.roll(lost, ROWS // 2, 0)), a[1] + b[1]

    def add_all(terms):
        while len(terms) > 1:
            terms = [add(*terms[i : i + 2]) if i + 1 < len(terms) else terms[i] for i in range(0, len(terms), 2)]
        return terms[0]

    beside = take_halo(2 * STEPS - 1, flat(ext_v, STEPS - 1), flat(ext_u, STEPS - 1))

    def hessian_level(l, carry):
        rh, hh, rg, gg = carry
        h = p_ref[l] + adjoint_of(STEPS - 1, l, beside)
        r = r_ref[l]
        g = h * SMALL
        h_ref[l] = h
        return add_product(rh, r, h), add_product(hh, h, h), rg + r * g, gg + g * g

    rh, hh, rg, gg = lax.fori_loop(0, L, hessian_level, ((zero, zero), (zero, zero), zero, zero), unroll=8)
    rr_high, rr_low = fold_rows(rr_part)
    rh_high, rh_low = fold_rows(rh)
    hh_high, hh_low = fold_rows(hh)
    pq_high, pq_low = fold_rows((pq_part, zero))
    parts = (rr_high, rh_high, hh_high, pq_high, rr_low, rh_low, hh_low, pq_low)
    tile = zero
    for i, part in enumerate(parts):
        tile = jnp.where(row == i, part, tile)
    rg, _ = fold_rows((rg, zero))
    gg, _ = fold_rows((gg, zero))
    red_send[0] = tile
    red_send[1] = jnp.where(row == 0, rg, gg)

    @pl.loop(0, PLANE - 1)
    def _(slot):
        plane_copy(slot).start()

    @pl.loop(0, PLANE - 1)
    def _(slot):
        plane_copy(slot).wait_recv()

    total = add_all(
        [(red_send[0], red_send[1])] + [(red_plane[i, 0], red_plane[i, 1]) for i in range(PLANE - 1)]
    )
    red_mid[0] = total[0]
    red_mid[1] = total[1]
    for dz in range(1, DEPTH):
        depth_copy(dz).start()
    for dz in range(1, DEPTH):
        depth_copy(dz).wait_recv()
    total = add_all([total] + [(red_depth[i, 0], red_depth[i, 1]) for i in range(DEPTH - 1)])
    for shift in (64, 32, 16, 8, 4, 2, 1):
        total = add(total, (pltpu.roll(total[0], shift, 1), pltpu.roll(total[1], shift, 1)))

    def at(tile, i):
        return jnp.broadcast_to(tile[i : i + 1], (ROWS, COLS))

    rr_high, rr_low = two_sum(at(total[0], 0), at(total[0], 4))
    rh_high, rh_low = two_sum(at(total[0], 1), at(total[0], 5))
    hh_high, hh_low = two_sum(at(total[0], 2), at(total[0], 6))
    alpha = rr_high / (at(total[0], 3) + at(total[0], 7))
    high, low = two_product(alpha, hh_high)
    high, lost = two_sum(2.0 * rh_high, -high)
    low = lost + (2.0 * rh_low - (low + alpha * hh_low))
    high, low = two_sum(high, low)
    after, rest = two_product(alpha, high)
    after, lost = two_sum(rr_high, -after)
    rr_next = after + (lost + (rr_low - (rest + alpha * low)))
    rg, gg = at(total[1], 0), at(total[1], 1)
    scaled = alpha * (1.0 / SMALL)
    rr_far = rr_high - scaled * (2.0 * rg - scaled * gg)
    rr_next = jnp.where(gg < 1e10, rr_next, rr_far)
    alpha_ref[...] = alpha
    beta_ref[...] = rr_next / rr_high

    for k in range(2 * STEPS):
        for copy in halo_copies(k):
            copy.wait_send()

    @pl.loop(0, PLANE - 1)
    def _(slot):
        for order in range(STEPS):
            weight_copy(order, slot, height_of(order)).wait_send()
        plane_copy(slot).wait_send()

    for dz in range(1, DEPTH):
        depth_copy(dz).wait_send()


def shards(increment, residual, direction, wind_east, wind_north, obs_column, obs_count, obs_weight):
    vmem = pl.BlockSpec(memory_space=pltpu.VMEM)
    dma = pltpu.SemaphoreType.DMA
    any_space = pl.BlockSpec(memory_space=pl.ANY)
    hessian, alpha, beta = pl.pallas_call(
        kernel,
        out_shape=(
            jax.ShapeDtypeStruct((L, ROWS, COLS), F32),
            jax.ShapeDtypeStruct((ROWS, COLS), F32),
            jax.ShapeDtypeStruct((ROWS, COLS), F32),
        ),
        in_specs=[any_space] * 7,
        out_specs=(vmem, vmem, vmem),
        scratch_shapes=[
            pltpu.VMEM((L, ROWS, COLS), F32),
            pltpu.VMEM((L, ROWS, COLS), F32),
            pltpu.VMEM((L, ROWS, COLS), F32),
            pltpu.VMEM((L, ROWS, COLS), F32),
            pltpu.VMEM((STEPS, PLANE * COLS), jnp.int32),
            pltpu.VMEM((STEPS, PLANE), jnp.int32),
            pltpu.VMEM((STEPS, PLANE, L + ROWS, COLS), F32),
            pltpu.VMEM((STEPS, PLANE, L + ROWS, COLS), F32),
            pltpu.VMEM((2 * L, CELLS), F32),
            pltpu.VMEM((L, ROWS, COLS), F32),
            pltpu.VMEM((STEPS + 1, LEVELS, PITCH, COLS), F32),
            pltpu.VMEM((STEPS, LEVELS, PITCH, COLS), F32),
            pltpu.VMEM((STEPS, LEVELS, PITCH, COLS), F32),
            pltpu.VMEM((STEPS, LEVELS, ROWS, COLS), F32),
            pltpu.VMEM((2 * STEPS, 2, L, COLS), F32),
            pltpu.VMEM((2 * STEPS, 2, L, COLS), F32),
            pltpu.VMEM((2 * STEPS, ROWS, COLS), F32),
            pltpu.VMEM((2 * STEPS, 2, ROWS, COLS), F32),
            pltpu.VMEM((2, ROWS, COLS), F32),
            pltpu.VMEM((PLANE - 1, 2, ROWS, COLS), F32),
            pltpu.VMEM((2, ROWS, COLS), F32),
            pltpu.VMEM((DEPTH - 1, 2, ROWS, COLS), F32),
            dma((6,)), dma((PLANE,)), dma((STEPS, PLANE)), dma((STEPS, PLANE)),
            dma((2 * STEPS, 4)), dma((2 * STEPS, 4)),
            dma((PLANE + DEPTH,)), dma((PLANE + DEPTH,)),
        ],
        compiler_params=pltpu.CompilerParams(
            collective_id=0, has_side_effects=True, vmem_limit_bytes=60 * 2**20
        ),
    )(direction, residual, wind_east, wind_north, obs_column, obs_count, obs_weight)
    new_increment = increment + alpha * direction
    new_residual = residual - alpha * hessian
    new_direction = new_residual + beta * direction
    return new_increment, new_residual, new_direction


def solution(mesh):
    field = P(None, "gy", "gx")
    slots = P(None, ("gy", "gx"))
    return jax.shard_map(
        shards,
        mesh=mesh,
        in_specs=(field, field, field, field, field, slots, slots, P(None, None, ("gy", "gx"))),
        out_specs=(field, field, field),
        check_vma=False,
    )
```

time: 106 us -> 94.3 us (0.89)
  local copies, waits for them, and re-layouts: 8.08 us -> 0.01 us
  Pallas kernels: 94.8 us -> 91.6 us
    unnamed x16 -> x6, local copies, waits for them, and re-layouts: 7.5 us -> 0.01 us
    pallas_call x1, Pallas kernels: 94.8 us -> 91.6 us  [shards(): pl.pallas_call(kernel, out_shape=(jax.ShapeDtypeStruct((L, ROWS, COLS), F...]
where the time goes in v1:
time: 94.3 us; the launch traced here: 94.2 us
  Pallas kernels  91.6 us (97%)
  other arithmetic  1.88 us (2%)
    pallas_call x1, Pallas kernels, shards(): pl.pallas_call(kernel, out_shape=(jax.ShapeDtypeStruct((L, ROWS, COLS), F...  91.6 us

profile of v1, /device:TPU:1, one launch (start us, length us, event | category | flops | bytes accessed | tf_op | source)
XLA Modules:
  0.0 94.2 jit_solution(7031069164862901317)
XLA Ops:
  0.6 0.0 copy-start
  0.6 0.0 copy-start.1
  0.7 0.0 copy-start.2
  0.7 91.6 %shard_map.103 = (f32[64,8,128]{2,1,0:T(8,128)}, f32[8,128]{1,0:T(8,128)}, f32[8,128]{1,0:T(8,128)}) custom-call(f32[64,8,128]{2,1,0:T(8,128)} %p_hbm.1, f32[64,8,128]{2,1,0:T(8,128)} %r_hbm.1, f32[64,8,128]{2,1,0:T(8,128)} %we_hbm.1, f32[64,8,128]{2,1,0:T(8,128)} %wn_hbm.1, s32[4,4096]{1,0:T(4,128)} %col_hbm.1, s32[4,32]{1,0:T(4,128)} %cnt_hbm.1, ...), custom_call_target="tpu_custom_call" | custom-call | tf_op jit(solution)/shard_map/pallas_call | solution.py:440
  92.3 0.0 copy-done
  92.3 0.0 copy-done.1
  92.3 0.0 copy-done.2
  92.3 1.9 %multiply_add_fusion = (f32[64,8,128]{2,1,0:T(8,128)}, f32[64,8,128]{2,1,0:T(8,128)}, f32[64,8,128]{2,1,0:T(8,128)}) fusion(f32[64,8,128]{2,1,0:T(8,128)S(1)} %copy-done, f32[8,128]{1,0:T(8,128)} %get-tuple-element.8, f32[64,8,128]{2,1,0:T(8,128)S(1)} %copy-done.1, f32[64,8,128]{2,1,0:T(8,128)} %get-tuple-element.7, f32[8,128]{1,0:T(8,128)} %get-tuple-element.6, ...), kind=kLoop, calls=%fused_computation | loop fusion | flops 393216 | bytes 1843200 | tf_op jit(solution)/shard_map/add | solution.py:482
Async XLA Ops:
  0.6 91.6 %copy-start = (f32[64,8,128]{2,1,0:T(8,128)S(1)}, f32[64,8,128]{2,1,0:T(8,128)}, u32[]{:S(2)}) copy-start(f32[64,8,128]{2,1,0:T(8,128)} %p_hbm.1) | copy-start | bytes 786436
  0.6 91.6 %copy-start.1 = (f32[64,8,128]{2,1,0:T(8,128)S(1)}, f32[64,8,128]{2,1,0:T(8,128)}, u32[]{:S(2)}) copy-start(f32[64,8,128]{2,1,0:T(8,128)} %r_hbm.1) | copy-start | bytes 786436
  0.7 91.6 %copy-start.2 = (f32[64,8,128]{2,1,0:T(8,128)S(1)}, f32[64,8,128]{2,1,0:T(8,128)}, u32[]{:S(2)}) copy-start(f32[64,8,128]{2,1,0:T(8,128)} %param.8) | copy-start | bytes 786436

commit v2 on v1

--- a/solution.py
+++ b/solution.py
@@ -20,7 +20,8 @@
 LEVELS = L + 2
 GROUP = 4
 CHUNKS = PLANE // GROUP
-OPENING = 10
+OPENING = 14
+STRIDE = 13
 SENDS = STEPS * (PLANE - 1)
 
 ADVECTION = 0.3
@@ -30,10 +31,8 @@
 
 
 def offset_of(slot):
-    def far_first(a):
-        return 2 - a + (a // 2) * (3 - 2 * (a % 2))
-
-    return far_first(slot // 8), far_first((slot // 2) % 4), 1 - slot % 2
+    o = STRIDE * (PLANE - 1 - slot) % PLANE
+    return o // 8, (o // 2) % 4, o % 2
 
 
 def peer_of(slot):
@@ -103,25 +102,18 @@
             (r_hbm, r_ref), (we_hbm, we_ref), (wn_hbm, wn_ref),
         ))
     ]
-    for load in loads:
+    weight_loads = [
+        pltpu.make_async_copy(w_hbm.at[t], w_send.at[t, pl.ds(0, L)], block_sem.at[t]) for t in range(STEPS)
+    ]
+    for load in loads[:3] + weight_loads[::-1] + loads[3:]:
         load.start()
 
-    def block_load(g):
-        here = pl.ds(pl.multiple_of(g * COLS, COLS), COLS)
-        return pltpu.make_async_copy(w_hbm.at[:, :, here], w_send.at[:, g, pl.ds(0, L)], block_sem.at[g])
-
-    @pl.loop(0, PLANE)
-    def _(g):
-        block_load(g).start()
-
     barrier = pltpu.get_barrier_semaphore()
 
-    @pl.loop(0, PLANE - 1)
-    def _(slot):
+    for slot in range(PLANE - 1):
         pl.semaphore_signal(barrier, inc=1, device_id={"gx": peer_of(slot)}, device_id_type=MESH)
 
-    @pl.loop(1, DEPTH)
-    def _(dz):
+    for dz in range(1, DEPTH):
         pl.semaphore_signal(barrier, inc=1, device_id={"gy": (gy + dz) % DEPTH}, device_id_type=MESH)
 
     loads[0].wait()
@@ -131,8 +123,9 @@
     for g in range(PLANE):
         live = slot_id < counts[:, g : g + 1]
         columns = jnp.where(live, col_ref[:, g * COLS : (g + 1) * COLS], -1).astype(F32)
-        w_send[STEPS - 1, g, L : L + STEPS, :] = columns
-        w_send[STEPS - 1, g, L + STEPS :, :] = columns
+        here = slice(g * COLS, (g + 1) * COLS)
+        w_send[STEPS - 1, L : L + STEPS, here] = columns
+        w_send[STEPS - 1, L + STEPS :, here] = columns
 
     for t in range(STEPS + 1):
         ext[t, 0] = jnp.zeros((PITCH, COLS), F32)
@@ -141,33 +134,28 @@
         abuf[s, 0] = jnp.zeros((ROWS, COLS), F32)
         abuf[s, LEVELS - 1] = jnp.zeros((ROWS, COLS), F32)
 
-    for load in loads[2:]:
-        load.wait()
+    loads[2].wait()
 
     def rolled_edges(field, l, acc):
         return jnp.where(pair == l, pltpu.roll(field, 2 * l + 1, 1), acc)
 
     def load_level(l, carry):
-        edges, rr, pp = carry
+        edges, pp = carry
         f = p_ref[l]
-        r = r_ref[l]
         ext[0, l + 1, 8:16, :] = f
-        return rolled_edges(f, l, edges), add_product(rr, r, r), pp + f * f
+        return rolled_edges(f, l, edges), pp + f * f
 
     zero = jnp.zeros((ROWS, COLS), F32)
-    edges, rr_part, pp_part = lax.fori_loop(0, L, load_level, (zero, (zero, zero), zero), unroll=8)
-
-    @pl.loop(0, PLANE)
-    def _(g):
-        block_load(g).wait()
-
+    edges, pp_part = lax.fori_loop(0, L, load_level, (zero, zero), unroll=8)
+
+    weight_loads[STEPS - 1].wait()
     pl.semaphore_wait(barrier, PLANE - 1 + DEPTH - 1)
 
     def weight_copy(order, slot, height):
         p = peer_of(slot)
         t = STEPS - 1 - order
         return pltpu.make_async_remote_copy(
-            src_ref=w_send.at[t, p, pl.ds(0, height)],
+            src_ref=w_send.at[t, pl.ds(0, height), pl.ds(pl.multiple_of(p * COLS, COLS), COLS)],
             dst_ref=w_recv.at[t, slot, pl.ds(0, height)],
             send_sem=w_ss.at[order, slot], recv_sem=w_rs.at[order, slot],
             device_id={"gx": p}, device_id_type=MESH,
@@ -224,6 +212,12 @@
         state = flat(ext, t - 1)
         send_halo(t - 1, state, state, edges)
         send_weights((t - 1) * OPENING, OPENING)
+        if t == 1:
+            for load in loads[3:] + weight_loads[: STEPS - 1]:
+                load.wait()
+            rr_part = lax.fori_loop(
+                0, L, lambda l, rr: add_product(rr, r_ref[l], r_ref[l]), (zero, zero), unroll=8
+            )
         beside = take_halo(t - 1, state, state)
 
         def tangent_level(l, edges, t=t, beside=beside):
@@ -252,7 +246,8 @@
         blocks = [w_recv.at[t, slot] for slot in slots]
         columns = [w_recv.at[STEPS - 1, slot] for slot in slots]
         if own:
-            blocks[-1], columns[-1] = w_send.at[t, me], w_send.at[STEPS - 1, me]
+            mine = pl.ds(pl.multiple_of(me * COLS, COLS), COLS)
+            blocks[-1], columns[-1] = w_send.at[t, :, mine], w_send.at[STEPS - 1, :, mine]
         weights = jnp.concatenate([block[:L, :] for block in blocks], axis=1)
         ids = jnp.concatenate([column[L + t : L + t + 1, :] for column in columns], axis=1)
         high = weights.astype(jnp.bfloat16)
@@ -345,8 +340,8 @@
     upper = row < ROWS // 2
 
     def add(a, b):
-        total, lost = two_sum(a[0], b[0])
-        return jnp.where(upper, total, total + pltpu.roll(lost, ROWS // 2, 0)), a[1] + b[1]
+        total, lost = two_sum(a, b)
+        return jnp.where(upper, total, total + pltpu.roll(lost, ROWS // 2, 0))
 
     def add_all(terms):
         while len(terms) > 1:
@@ -374,37 +369,34 @@
         tile = jnp.where(row == i, part, tile)
     rg, _ = fold_rows((rg, zero))
     gg, _ = fold_rows((gg, zero))
-    red_send[0] = tile
-    red_send[1] = jnp.where(row == 0, rg, gg)
-
-    @pl.loop(0, PLANE - 1)
-    def _(slot):
+    far = jnp.where(row == 0, rg, jnp.where(row == 1, gg, 0.0))
+    half = COLS // 2
+    tile = add(tile, pltpu.roll(tile, half, 1))
+    far = add(far, pltpu.roll(far, half, 1))
+    red_send[...] = jnp.where(lane < half, tile, far)
+
+    for slot in range(PLANE - 1):
         plane_copy(slot).start()
-
-    @pl.loop(0, PLANE - 1)
-    def _(slot):
+    for slot in range(PLANE - 1):
         plane_copy(slot).wait_recv()
 
-    total = add_all(
-        [(red_send[0], red_send[1])] + [(red_plane[i, 0], red_plane[i, 1]) for i in range(PLANE - 1)]
-    )
-    red_mid[0] = total[0]
-    red_mid[1] = total[1]
+    total = add_all([red_send[...]] + [red_plane[i] for i in range(PLANE - 1)])
+    red_mid[...] = total
     for dz in range(1, DEPTH):
         depth_copy(dz).start()
     for dz in range(1, DEPTH):
         depth_copy(dz).wait_recv()
-    total = add_all([total] + [(red_depth[i, 0], red_depth[i, 1]) for i in range(DEPTH - 1)])
-    for shift in (64, 32, 16, 8, 4, 2, 1):
-        total = add(total, (pltpu.roll(total[0], shift, 1), pltpu.roll(total[1], shift, 1)))
-
-    def at(tile, i):
-        return jnp.broadcast_to(tile[i : i + 1], (ROWS, COLS))
-
-    rr_high, rr_low = two_sum(at(total[0], 0), at(total[0], 4))
-    rh_high, rh_low = two_sum(at(total[0], 1), at(total[0], 5))
-    hh_high, hh_low = two_sum(at(total[0], 2), at(total[0], 6))
-    alpha = rr_high / (at(total[0], 3) + at(total[0], 7))
+    total = add_all([total] + [red_depth[i] for i in range(DEPTH - 1)])
+    for shift in (32, 16, 8, 4, 2, 1):
+        total = add(total, pltpu.roll(total, COLS - shift, 1))
+
+    def at(i, first=0):
+        return jnp.broadcast_to(total[i : i + 1, first : first + 1], (ROWS, COLS))
+
+    rr_high, rr_low = two_sum(at(0), at(4))
+    rh_high, rh_low = two_sum(at(1), at(5))
+    hh_high, hh_low = two_sum(at(2), at(6))
+    alpha = rr_high / (at(3) + at(7))
     high, low = two_product(alpha, hh_high)
     high, lost = two_sum(2.0 * rh_high, -high)
     low = lost + (2.0 * rh_low - (low + alpha * hh_low))
@@ -412,7 +404,7 @@
     after, rest = two_product(alpha, high)
     after, lost = two_sum(rr_high, -after)
     rr_next = after + (lost + (rr_low - (rest + alpha * low)))
-    rg, gg = at(total[1], 0), at(total[1], 1)
+    rg, gg = at(0, half), at(1, half)
     scaled = alpha * (1.0 / SMALL)
     rr_far = rr_high - scaled * (2.0 * rg - scaled * gg)
     rr_next = jnp.where(gg < 1e10, rr_next, rr_far)
@@ -453,7 +445,7 @@
             pltpu.VMEM((L, ROWS, COLS), F32),
             pltpu.VMEM((STEPS, PLANE * COLS), jnp.int32),
             pltpu.VMEM((STEPS, PLANE), jnp.int32),
-            pltpu.VMEM((STEPS, PLANE, L + ROWS, COLS), F32),
+            pltpu.VMEM((STEPS, L + ROWS, PLANE * COLS), F32),
             pltpu.VMEM((STEPS, PLANE, L + ROWS, COLS), F32),
             pltpu.VMEM((2 * L, CELLS), F32),
             pltpu.VMEM((L, ROWS, COLS), F32),
@@ -465,11 +457,11 @@
             pltpu.VMEM((2 * STEPS, 2, L, COLS), F32),
             pltpu.VMEM((2 * STEPS, ROWS, COLS), F32),
             pltpu.VMEM((2 * STEPS, 2, ROWS, COLS), F32),
-            pltpu.VMEM((2, ROWS, COLS), F32),
-            pltpu.VMEM((PLANE - 1, 2, ROWS, COLS), F32),
-            pltpu.VMEM((2, ROWS, COLS), F32),
-            pltpu.VMEM((DEPTH - 1, 2, ROWS, COLS), F32),
-            dma((6,)), dma((PLANE,)), dma((STEPS, PLANE)), dma((STEPS, PLANE)),
+            pltpu.VMEM((ROWS, COLS), F32),
+            pltpu.VMEM((PLANE - 1, ROWS, COLS), F32),
+            pltpu.VMEM((ROWS, COLS), F32),
+            pltpu.VMEM((DEPTH - 1, ROWS, COLS), F32),
+            dma((6,)), dma((STEPS,)), dma((STEPS, PLANE)), dma((STEPS, PLANE)),
             dma((2 * STEPS, 4)), dma((2 * STEPS, 4)),
             dma((PLANE + DEPTH,)), dma((PLANE + DEPTH,)),
         ],

time: 94.3 us -> 86.4 us (0.916)
  Pallas kernels: 91.6 us -> 83.7 us
    pallas_call x1, Pallas kernels: 91.6 us -> 83.7 us  [shards(): pl.pallas_call(kernel, out_shape=(jax.ShapeDtypeStruct((L, ROWS, COLS), F...]
where the time goes in v2:
time: 86.4 us; the launch traced here: 86.3 us
  Pallas kernels  83.7 us (97%)
  other arithmetic  1.88 us (2%)
    pallas_call x1, Pallas kernels, shards(): pl.pallas_call(kernel, out_shape=(jax.ShapeDtypeStruct((L, ROWS, COLS), F...  83.7 us
    add x1, other arithmetic, shards(): new_direction = new_residual + beta * direction  1.88 us

profile of v2, /device:TPU:1, one launch (start us, length us, event | category | flops | bytes accessed | tf_op | source)
XLA Modules:
  0.0 86.3 jit_solution(6000682854790049184)
XLA Ops:
  0.6 0.0 copy-start
  0.6 0.0 copy-start.1
  0.7 0.0 copy-start.2
  0.7 83.7 %shard_map.103 = (f32[64,8,128]{2,1,0:T(8,128)}, f32[8,128]{1,0:T(8,128)}, f32[8,128]{1,0:T(8,128)}) custom-call(f32[64,8,128]{2,1,0:T(8,128)} %p_hbm.1, f32[64,8,128]{2,1,0:T(8,128)} %r_hbm.1, f32[64,8,128]{2,1,0:T(8,128)} %we_hbm.1, f32[64,8,128]{2,1,0:T(8,128)} %wn_hbm.1, s32[4,4096]{1,0:T(4,128)} %col_hbm.1, s32[4,32]{1,0:T(4,128)} %cnt_hbm.1, ...), custom_call_target="tpu_custom_call" | custom-call | tf_op jit(solution)/shard_map/pallas_call | solution.py:432
  84.4 0.0 copy-done
  84.4 0.0 copy-done.1
  84.4 0.0 copy-done.2
  84.4 1.9 %multiply_add_fusion = (f32[64,8,128]{2,1,0:T(8,128)}, f32[64,8,128]{2,1,0:T(8,128)}, f32[64,8,128]{2,1,0:T(8,128)}) fusion(f32[64,8,128]{2,1,0:T(8,128)S(1)} %copy-done, f32[8,128]{1,0:T(8,128)} %get-tuple-element.8, f32[64,8,128]{2,1,0:T(8,128)S(1)} %copy-done.1, f32[64,8,128]{2,1,0:T(8,128)} %get-tuple-element.7, f32[8,128]{1,0:T(8,128)} %get-tuple-element.6, ...), kind=kLoop, calls=%fused_computation | loop fusion | flops 393216 | bytes 1843200 | tf_op jit(solution)/shard_map/add | solution.py:474
Async XLA Ops:
  0.6 83.7 %copy-start = (f32[64,8,128]{2,1,0:T(8,128)S(1)}, f32[64,8,128]{2,1,0:T(8,128)}, u32[]{:S(2)}) copy-start(f32[64,8,128]{2,1,0:T(8,128)} %p_hbm.1) | copy-start | bytes 786436
  0.6 83.7 %copy-start.1 = (f32[64,8,128]{2,1,0:T(8,128)S(1)}, f32[64,8,128]{2,1,0:T(8,128)}, u32[]{:S(2)}) copy-start(f32[64,8,128]{2,1,0:T(8,128)} %r_hbm.1) | copy-start | bytes 786436
  0.7 83.7 %copy-start.2 = (f32[64,8,128]{2,1,0:T(8,128)S(1)}, f32[64,8,128]{2,1,0:T(8,128)}, u32[]{:S(2)}) copy-start(f32[64,8,128]{2,1,0:T(8,128)} %param.8) | copy-start | bytes 786436

commit v3 on v2

--- a/solution.py
+++ b/solution.py
@@ -377,6 +377,15 @@
 
     for slot in range(PLANE - 1):
         plane_copy(slot).start()
+    for k in range(2 * STEPS):
+        for copy in halo_copies(k):
+            copy.wait_send()
+
+    @pl.loop(0, PLANE - 1)
+    def _(slot):
+        for order in range(STEPS):
+            weight_copy(order, slot, height_of(order)).wait_send()
+
     for slot in range(PLANE - 1):
         plane_copy(slot).wait_recv()
 
@@ -384,6 +393,8 @@
     red_mid[...] = total
     for dz in range(1, DEPTH):
         depth_copy(dz).start()
+    for slot in range(PLANE - 1):
+        plane_copy(slot).wait_send()
     for dz in range(1, DEPTH):
         depth_copy(dz).wait_recv()
     total = add_all([total] + [red_depth[i] for i in range(DEPTH - 1)])
@@ -410,16 +421,6 @@
     rr_next = jnp.where(gg < 1e10, rr_next, rr_far)
     alpha_ref[...] = alpha
     beta_ref[...] = rr_next / rr_high
-
-    for k in range(2 * STEPS):
-        for copy in halo_copies(k):
-            copy.wait_send()
-
-    @pl.loop(0, PLANE - 1)
-    def _(slot):
-        for order in range(STEPS):
-            weight_copy(order, slot, height_of(order)).wait_send()
-        plane_copy(slot).wait_send()
 
     for dz in range(1, DEPTH):
         depth_copy(dz).wait_send()

time: 86.4 us -> 86 us (level)
  no operation moved by 1% of the time
where the time goes in v3:
time: 86 us; the launch traced here: 85.9 us
  Pallas kernels  83.3 us (97%)
  other arithmetic  1.88 us (2%)
    pallas_call x1, Pallas kernels, shards(): pl.pallas_call(kernel, out_shape=(jax.ShapeDtypeStruct((L, ROWS, COLS), F...  83.3 us
    add x1, other arithmetic, shards(): new_direction = new_residual + beta * direction  1.88 us

profile of v3, /device:TPU:1, one launch (start us, length us, event | category | flops | bytes accessed | tf_op | source)
XLA Modules:
  0.0 85.9 jit_solution(16599276189371337894)
XLA Ops:
  0.6 0.0 copy-start
  0.6 0.0 copy-start.1
  0.7 0.0 copy-start.2
  0.7 83.3 %shard_map.103 = (f32[64,8,128]{2,1,0:T(8,128)}, f32[8,128]{1,0:T(8,128)}, f32[8,128]{1,0:T(8,128)}) custom-call(f32[64,8,128]{2,1,0:T(8,128)} %p_hbm.1, f32[64,8,128]{2,1,0:T(8,128)} %r_hbm.1, f32[64,8,128]{2,1,0:T(8,128)} %we_hbm.1, f32[64,8,128]{2,1,0:T(8,128)} %wn_hbm.1, s32[4,4096]{1,0:T(4,128)} %col_hbm.1, s32[4,32]{1,0:T(4,128)} %cnt_hbm.1, ...), custom_call_target="tpu_custom_call" | custom-call | tf_op jit(solution)/shard_map/pallas_call | solution.py:433
  84.0 0.0 copy-done
  84.0 0.0 copy-done.1
  84.0 0.0 copy-done.2
  84.0 1.9 %multiply_add_fusion = (f32[64,8,128]{2,1,0:T(8,128)}, f32[64,8,128]{2,1,0:T(8,128)}, f32[64,8,128]{2,1,0:T(8,128)}) fusion(f32[64,8,128]{2,1,0:T(8,128)S(1)} %copy-done, f32[8,128]{1,0:T(8,128)} %get-tuple-element.8, f32[64,8,128]{2,1,0:T(8,128)S(1)} %copy-done.1, f32[64,8,128]{2,1,0:T(8,128)} %get-tuple-element.7, f32[8,128]{1,0:T(8,128)} %get-tuple-element.6, ...), kind=kLoop, calls=%fused_computation | loop fusion | flops 393216 | bytes 1843200 | tf_op jit(solution)/shard_map/add | solution.py:475
Async XLA Ops:
  0.6 83.4 %copy-start = (f32[64,8,128]{2,1,0:T(8,128)S(1)}, f32[64,8,128]{2,1,0:T(8,128)}, u32[]{:S(2)}) copy-start(f32[64,8,128]{2,1,0:T(8,128)} %p_hbm.1) | copy-start | bytes 786436
  0.6 83.4 %copy-start.1 = (f32[64,8,128]{2,1,0:T(8,128)S(1)}, f32[64,8,128]{2,1,0:T(8,128)}, u32[]{:S(2)}) copy-start(f32[64,8,128]{2,1,0:T(8,128)} %r_hbm.1) | copy-start | bytes 786436
  0.7 83.4 %copy-start.2 = (f32[64,8,128]{2,1,0:T(8,128)S(1)}, f32[64,8,128]{2,1,0:T(8,128)}, u32[]{:S(2)}) copy-start(f32[64,8,128]{2,1,0:T(8,128)} %param.8) | copy-start | bytes 786436
